TPU v7x, 512 devices: a whole 4x4x16 slice. The times are simulated.
512 devices in a mesh: segment: 4 (over y_lo, core), ctx: 32 (over z, y_hi), head: 4 (over x).
Axes of the slice: x: 4, y: 4 (y_hi: 2, y_lo: 2; y = y_hi * 2 + y_lo), z: 16, core: 2. Of those that a mesh axis runs over, the one named last changes fastest.
Arguments:
- hidden: bfloat16 [4, 8192, 2880], P('segment', 'ctx', 'head'), may hold values from -450 to 450
- merge_weight: bfloat16 [3, 2880, 2880], P(None, 'head', 'segment'), may hold values from -0.0625 to 0.0625
- query_weight: bfloat16 [5760, 2048], P('ctx', ('segment', 'head')), may hold values from -1 to 1
- key_weight: bfloat16 [5760, 256], P('ctx', 'segment'), may hold values from -8 to 8
- value_weight: bfloat16 [5760, 256], P('ctx', 'segment'), may hold values from -0.078125 to 0.078125
- block_order: int32 [64], replicated, may hold values from 0 to 63, each once
Outputs:
- attended: bfloat16 [8192, 2048], P('ctx', ('segment', 'head'))
Inputs may be any that keep to these rules, and one draw needn't show every extreme that they name: `block_order`: a permutation of the sequence blocks.
All inputs are finite; a program needn't handle non-finite values.
Results may differ from a plain program's by a relative error of at most 0.023.
The roundings to bfloat16 on the way count: a program that leaves them out, or rounds other values in their place, can miss the bound.
Values may be sent and summed in bfloat16 or wider, within the bound.
No kernel may reach another device: no remote copies, remote signals or barrier semaphores. Data moves between devices by JAX's collectives and lax.ppermute only.
A program may use at most 64 MiB of HBM per device.

v0:
```python
import math
import jax
import jax.numpy as jnp
from jax import lax
from jax.sharding import PartitionSpec as P

HD = 64


def normalize(matrix):
    widened = matrix.astype(jnp.float32)
    return widened * lax.rsqrt(jnp.mean(widened * widened, axis=-1, keepdims=True) + 1e-06)


def seq_positions(row_ids, order, block_len):
    block_ids = jnp.arange(order.shape[0], dtype=jnp.int32)
    matches = (row_ids // block_len)[:, None] == block_ids[None, :]
    block_first = jnp.sum(jnp.where(matches, order[None, :], 0), axis=1)
    return block_first * block_len + row_ids % block_len


def attend_block(carry, query_heads, query_pos, key_blk, value_blk, key_pos):
    run_max, run_total, accum = carry
    tok_rows, heads_count, head_size = query_heads.shape
    scores = (
        jnp.einsum("tgd,nd->tgn", query_heads, key_blk, preferred_element_type=jnp.float32) * 0.125
    )
    allowed = key_pos[None, None, :] <= query_pos[:, None, None]
    scores = jnp.where(allowed, scores, -1e30)
    new_max = jnp.maximum(run_max, jnp.max(scores, axis=2))
    rescale = jnp.exp(run_max - new_max)
    unscaled = jnp.where(allowed, jnp.exp(scores - new_max[:, :, None]), 0.0)
    run_total = run_total * rescale + jnp.sum(unscaled, axis=2)
    mixed_rows = jnp.einsum(
        "tgn,nd->tgd", unscaled.astype(jnp.bfloat16), value_blk, preferred_element_type=jnp.float32
    )
    grown = accum.reshape(tok_rows, heads_count, head_size) * rescale[:, :, None] + mixed_rows
    return (new_max, run_total, grown.reshape(tok_rows, heads_count * head_size))


def body(hidden, merge_weight, query_weight, key_weight, value_weight, block_order):
    tok_rows = hidden.shape[1]
    block_len = tok_rows // 2
    segments = lax.axis_size("segment")
    heads_here = lax.axis_size("head")
    segment_id = lax.axis_index("segment")
    head_id = lax.axis_index("head")
    ctx_id = lax.axis_index("ctx")
    sections = lax.all_gather(hidden, "segment", axis=0, tiled=True)
    partial_value = jnp.einsum(
        "ktf,kfc->tc", sections[:3], merge_weight, preferred_element_type=jnp.float32
    )
    col_piece = partial_value.shape[1] // heads_here
    summed = lax.psum(partial_value, "head")
    merged_part = lax.dynamic_slice_in_dim(summed, head_id * col_piece, col_piece, 1)
    merged_part = merged_part.astype(jnp.bfloat16)
    embed_part = lax.dynamic_slice_in_dim(sections[3], segment_id * col_piece, col_piece, 1)
    merged_all, embed_mixed = (
        lax.all_gather(merged_part, ("segment", "head"), axis=1, tiled=True),
        lax.all_gather(embed_part, ("segment", "head"), axis=1, tiled=True),
    )
    embed_all = embed_mixed.reshape(tok_rows, segments, heads_here, col_piece).transpose(0, 2, 1, 3)
    embed_all = embed_all.reshape(tok_rows, segments * heads_here * col_piece)
    draft_input = jnp.concatenate([normalize(embed_all), normalize(merged_all)], axis=1).astype(
        jnp.bfloat16
    )
    query_piece = lax.all_gather(query_weight, "ctx", axis=0, tiled=True)
    key_piece = lax.all_gather(key_weight, "ctx", axis=0, tiled=True)
    value_piece = lax.all_gather(value_weight, "ctx", axis=0, tiled=True)
    query_acc = jnp.dot(draft_input, query_piece, preferred_element_type=jnp.float32)
    key_acc = jnp.dot(draft_input, key_piece, preferred_element_type=jnp.float32)
    value_acc = jnp.dot(draft_input, value_piece, preferred_element_type=jnp.float32)
    query_acc, key_acc, value_acc = (query_acc, key_acc, value_acc)
    query_heads = query_acc.astype(jnp.bfloat16).reshape(tok_rows, -1, HD)
    key_vectors = key_acc.astype(jnp.bfloat16)
    value_vectors = value_acc.astype(jnp.bfloat16)
    heads_count = query_heads.shape[1]
    query_pos = seq_positions(
        ctx_id * tok_rows + jnp.arange(tok_rows, dtype=jnp.int32), block_order, block_len
    )
    initial_attn = (
        jnp.full((tok_rows, heads_count), -1e30, jnp.float32),
        jnp.zeros((tok_rows, heads_count), jnp.float32),
        jnp.zeros((tok_rows, heads_count * HD), jnp.float32),
    )
    key_piece = lax.all_gather(key_vectors, "ctx", axis=0, tiled=True)
    value_piece = lax.all_gather(value_vectors, "ctx", axis=0, tiled=True)
    row_count = key_piece.shape[0]
    key_step = math.gcd(row_count, 512)

    def one_block(turn_index, carried):
        offset = turn_index * key_step
        key_blk = lax.dynamic_slice_in_dim(key_piece, offset, key_step, 0)
        value_blk = lax.dynamic_slice_in_dim(value_piece, offset, key_step, 0)
        key_pos = seq_positions(
            offset + jnp.arange(key_step, dtype=jnp.int32), block_order, block_len
        )
        return attend_block(carried, query_heads, query_pos, key_blk, value_blk, key_pos)

    run_max, run_total, accum = lax.fori_loop(0, row_count // key_step, one_block, initial_attn)
    output = accum.reshape(tok_rows, heads_count, HD) / run_total[:, :, None]
    return output.reshape(tok_rows, heads_count * HD).astype(jnp.bfloat16)


def solution(mesh):
    return jax.shard_map(
        body,
        mesh=mesh,
        in_specs=(
            P("segment", "ctx", "head"),
            P(None, "head", "segment"),
            P("ctx", ("segment", "head")),
            P("ctx", "segment"),
            P("ctx", "segment"),
            P(),
        ),
        out_specs=P("ctx", ("segment", "head")),
        check_vma=False,
    )
```

profile of v0, /device:TPU:4, one launch (start us, length us, event | category | flops | bytes accessed | tf_op | source)
XLA Modules:
  0.0 691.7 jit_solution(7909298819602587909)
XLA Ops:
  7.3 38.2 %all-gather.12.cloned.1.call-done = bf16[4,256,720]{1,2,0:T(8,128)(2,1)} async-done(((bf16[1,256,720]{1,2,0:T(8,128)(2,1)}), bf16[4,256,720]{1,2,0:T(8,128)(2,1)}) %all-gather.12.cloned.1.call-update) | async-done | bytes 1474576 | tf_op jit(solution)/shard_map/all_gather | solution.py:49
  47.5 3.6 convolution_bitcast_fusion
  51.1 25.7 %all-reduce.1 = bf16[256,720]{0,1:T(8,128)(2,1)} all-reduce(f32[256,720]{0,1:T(8,128)} %convolution_bitcast_fusion), channel_id=1, replica_groups=mesh['segment'=4,'ctx'=32,'head'=4] {'head'}, use_global_device_ids=true, to_apply=%region_1.0 | all-reduce | flops 184320 | bytes 1105920 | tf_op jit(solution)/shard_map/psum | solution.py:54
  79.0 83.5 %all-gather.4 = bf16[32,180,64]{1,2,0:T(8,128)(2,1)S(1)} all-gather(bf16[1,180,64]{1,2,0:T(8,128)(2,1)S(1)} %bitcast.59), channel_id=1, replica_groups=mesh['segment'=4,'ctx'=32,'head'=4] {'ctx'}, dimensions={0}, use_global_device_ids=true | all-gather | bytes 760320 | tf_op jit(solution)/shard_map/all_gather | solution.py:69
  164.1 3.1 reshape.158
  167.2 31.9 %multiply_reduce_fusion.1 = (f32[256]{0:T(256)S(1)}, f32[256,2880]{0,1:T(8,128)}) fusion(bf16[1,256,2880]{1,0,2:T(2,128)(2,1)} %all-gather.18.cloned.1.call-done), kind=kLoop, calls=%fused_computation.39 | loop fusion | flops 2211584 | bytes 4424704 | tf_op jit(solution)/shard_map/reduce_sum | solution.py:12
  199.1 4.0 reshape.145
  203.2 3.8 copy.26
  207.0 4.1 reshape.144
  211.1 3.4 reshape.159
  214.5 2.4 multiply_reduce_fusion
  222.4 78.1 %all-gather.2 = bf16[32,180,64]{1,2,0:T(8,128)(2,1)S(1)} all-gather(bf16[1,180,64]{1,2,0:T(8,128)(2,1)S(1)} %bitcast.60), channel_id=1, replica_groups=mesh['segment'=4,'ctx'=32,'head'=4] {'ctx'}, dimensions={0}, use_global_device_ids=true | all-gather | bytes 760320 | tf_op jit(solution)/shard_map/all_gather | solution.py:68
  302.0 3.2 reshape.154
  305.2 3.3 convolution_convert_fusion.2
  308.7 9.7 %all-gather.22.cloned.1.call-done = bf16[32,180,128]{2,1,0:T(8,128)(2,1)} async-done(((bf16[1,180,128]{2,1,0:T(8,128)(2,1)}), bf16[32,180,128]{2,1,0:T(8,128)(2,1)}) %all-gather.22.cloned.1.call-update) | async-done | bytes 1474576 | tf_op jit(solution)/shard_map/all_gather | solution.py:67
  318.4 3.3 reshape.156
  321.7 3.0 convolution_convert_fusion
  324.7 127.4 %all-gather.16.cloned.1.call-done = bf16[8192,64]{0,1:T(8,128)(2,1)} async-done(((bf16[256,64]{0,1:T(8,128)(2,1)}), bf16[8192,64]{0,1:T(8,128)(2,1)}) %all-gather.16.cloned.1.call-update) | async-done | bytes 1048592 | tf_op jit(solution)/shard_map/all_gather | solution.py:87
  452.1 132.5 %all-gather.14.cloned.1.call-done = bf16[8192,64]{0,1:T(8,128)(2,1)} async-done(((bf16[256,64]{0,1:T(8,128)(2,1)}), bf16[8192,64]{0,1:T(8,128)(2,1)}) %all-gather.14.cloned.1.call-update) | async-done | bytes 1048592 | tf_op jit(solution)/shard_map/all_gather | solution.py:86
  585.3 98.0 %while.20 = (s32[]{:T(128)}, f32[256,2]{0,1:T(2,128)S(1)}, f32[256,2]{0,1:T(2,128)S(1)}, f32[256,128]{0,1:T(8,128)}, s32[64]{0:T(128)S(1)}, /*index=5*/s32[256]{...) while((s32[]{:T(128)}, f32[256,2]{0,1:T(2,128)S(1)}, ...), condition=%wide.region_8.9_spmd.clone, body=%wide.region_4.8_spmd.clone.sunk | while | flops 69780480 | bytes 4175302 | solution.py:100
  607.6 2.2 convolution_add_fusion.2
  632.1 2.2 convolution_add_fusion.2
  656.5 2.2 convolution_add_fusion.2
  681.0 2.2 convolution_add_fusion.2
  (207 shorter events, 104.7 us)
Async XLA Ops:
  6.5 41.0 %copy-start = (bf16[3,720,720]{2,1,0:T(8,128)(2,1)S(1)}, bf16[3,720,720]{2,1,0:T(8,128)(2,1)}, u32[]{:S(2)}) copy-start(bf16[3,720,720]{2,1,0:T(8,128)(2,1)} %param.9) | copy-start | bytes 9331204
  6.5 39.0 %all-gather.12.cloned.1.call-start = ((), (), s32[]{:S(2)}) async-start(), calls=%async_computation | async-start | bytes 1843200 | tf_op jit(solution)/shard_map/all_gather | solution.py:49
  7.3 160.0 %all-gather.18.cloned.1.call-start = ((), (), s32[]{:S(2)}) async-start(), calls=%async_computation.3 | async-start | bytes 3133440 | tf_op jit(solution)/shard_map/all_gather | solution.py:60
  47.4 163.6 %all-gather.20.cloned.1.call-start = ((), (), s32[]{:S(2)}) async-start(), calls=%async_computation.4 | async-start | bytes 1601536 | tf_op jit(solution)/shard_map/all_gather | solution.py:59
  47.5 31.5 %copy-start.6 = (bf16[180,64]{0,1:T(8,128)(2,1)S(1)}, bf16[180,64]{0,1:T(8,128)(2,1)}, u32[]{:S(2)}) copy-start(bf16[180,64]{0,1:T(8,128)(2,1)} %param.12) | copy-start | bytes 69124
  78.3 240.1 %all-gather.22.cloned.1.call-start = ((), (), s32[]{:S(2)}) async-start(), calls=%async_computation.5 | async-start | bytes 1554432 | tf_op jit(solution)/shard_map/all_gather | solution.py:67
  78.9 373.2 %all-gather.16.cloned.1.call-start = ((), (), s32[]{:S(2)}) async-start(), calls=%async_computation.2 | async-start | bytes 1081344 | tf_op jit(solution)/shard_map/all_gather | solution.py:87
  214.5 2.7 copy-start.1
  216.9 1.9 copy-start.2
  218.8 1.1 copy-start.3
  218.8 2.2 copy-start.5
  219.9 1.1 copy-start.4
  221.0 1.3 copy-start.7
  222.3 362.3 %all-gather.14.cloned.1.call-start = ((), (), s32[]{:S(2)}) async-start(), calls=%async_computation.1 | async-start | bytes 1081344 | tf_op jit(solution)/shard_map/all_gather | solution.py:86
  305.2 3.4 copy-start.8
Sparse Core Ops, SparseCore 0:
  9.5 36.0 all-gather.11
  47.6 58.5 all-gather.17
  108.3 56.1 all-gather.19
  167.5 150.8 all-gather.21
  321.1 130.8 all-gather.15
  454.9 129.7 all-gather.13
where the time goes:
time: 694 us; the launch traced here: 692 us
  waiting for transfers between devices  309 us (45%)
  blocking collectives  187 us (27%)
  matrix products  81 us (12%)
  other arithmetic  63.7 us (9%)
  local copies, waits for them, and re-layouts  36.5 us (5%)
  between operations  13.6 us (2%)
    all_gather x1, waiting for transfers between devices, body(): key_piece = lax.all_gather(key_vectors, 'ctx', axis=0, tiled=True)  133 us
    all_gather x1, waiting for transfers between devices, body(): value_piece = lax.all_gather(value_vectors, 'ctx', axis=0, tiled=True)  127 us
    all_gather x1, blocking collectives, body(): value_piece = lax.all_gather(value_weight, 'ctx', axis=0, tiled=True)  83.5 us
    all_gather x1, blocking collectives, body(): key_piece = lax.all_gather(key_weight, 'ctx', axis=0, tiled=True)  78.1 us
    all_gather x1, waiting for transfers between devices, body(): sections = lax.all_gather(hidden, 'segment', axis=0, tiled=True)  38.2 us
    dot_general x16, matrix products, attend_block(): jnp.einsum('tgn,nd->tgd', unscaled.astype(jnp.bfloat16), value_blk, prefe...  35.4 us
    dot_general x16, matrix products, attend_block(): jnp.einsum('tgd,nd->tgn', query_heads, key_blk, preferred_element_type=jn...  34.5 us
    reduce_sum x2, other arithmetic, normalize(): jnp.mean(widened * widened, axis=-1, keepdims=True) + 1e-06  34.3 us
  transfers between devices with their start and end apart: 6, of which 4 were waited for; matrix products, arithmetic and copies ran while one was open for 11% of the time, Pallas kernels for 0%

commit v1 on v0

--- a/solution.py
+++ b/solution.py
@@ -65,7 +65,9 @@
         jnp.bfloat16
     )
     query_piece = lax.all_gather(query_weight, "ctx", axis=0, tiled=True)
-    key_piece = lax.all_gather(key_weight, "ctx", axis=0, tiled=True)
+    key_piece = jnp.concatenate(
+        lax.all_to_all(jnp.stack([key_weight] * lax.axis_size("ctx")), "ctx", 0, 0), axis=0
+    )
     value_piece = lax.all_gather(value_weight, "ctx", axis=0, tiled=True)
     query_acc = jnp.dot(draft_input, query_piece, preferred_element_type=jnp.float32)
     key_acc = jnp.dot(draft_input, key_piece, preferred_element_type=jnp.float32)

time: 694 us -> 720 us (1.037)
  waiting for transfers between devices: 309 us -> 364 us
  blocking collectives: 187 us -> 140 us
  starting transfers between devices: 0.21 us -> 15.3 us
    all_gather x1 -> x0, blocking collectives: 78.1 us -> none  [body(): key_piece = lax.all_gather(key_weight, 'ctx', axis=0, tiled=True)]
    all_gather x1, waiting for transfers between devices: 9.71 us -> 65.8 us  [body(): query_piece = lax.all_gather(query_weight, 'ctx', axis=0, tiled=True)]
    all_gather x1, blocking collectives: 83.5 us -> 115 us  [body(): value_piece = lax.all_gather(value_weight, 'ctx', axis=0, tiled=True)]
    all_to_all x0 -> x1, starting transfers between devices: none -> 14.9 us  [body(): lax.all_to_all(jnp.stack([key_weight] * lax.axis_size('ctx')), 'ctx', 0, 0)]
    unnamed x22 -> x19, local copies, waits for them, and re-layouts: 14.8 us -> 9.11 us
  transfers between devices with their start and end apart: 6 -> 7, of which waited for: 4 -> 4; matrix products, arithmetic and copies ran while one was open for 11% -> 11% of each run, Pallas kernels for 0% -> 0%
where the time goes in v1:
time: 720 us; the launch traced here: 718 us
  waiting for transfers between devices  364 us (51%)
  blocking collectives  140 us (19%)
  matrix products  80.8 us (11%)
  other arithmetic  66.8 us (9%)
  local copies, waits for them, and re-layouts  36.4 us (5%)
  starting transfers between devices  15.3 us (2%)
  between operations  13.6 us (2%)
    all_gather x1, waiting for transfers between devices, body(): key_piece = lax.all_gather(key_vectors, 'ctx', axis=0, tiled=True)  133 us
    all_gather x1, waiting for transfers between devices, body(): value_piece = lax.all_gather(value_vectors, 'ctx', axis=0, tiled=True)  127 us
    all_gather x1, blocking collectives, body(): value_piece = lax.all_gather(value_weight, 'ctx', axis=0, tiled=True)  115 us
    all_gather x1, waiting for transfers between devices, body(): query_piece = lax.all_gather(query_weight, 'ctx', axis=0, tiled=True)  65.8 us
    all_gather x1, waiting for transfers between devices, body(): sections = lax.all_gather(hidden, 'segment', axis=0, tiled=True)  38.2 us
    dot_general x16, matrix products, attend_block(): jnp.einsum('tgn,nd->tgd', unscaled.astype(jnp.bfloat16), value_blk, prefe...  35.6 us
    reduce_sum x2, other arithmetic, normalize(): jnp.mean(widened * widened, axis=-1, keepdims=True) + 1e-06  34.3 us
    dot_general x16, matrix products, attend_block(): jnp.einsum('tgd,nd->tgn', query_heads, key_blk, preferred_element_type=jn...  34.1 us
  transfers between devices with their start and end apart: 7, of which 4 were waited for; matrix products, arithmetic and copies ran while one was open for 11% of the time, Pallas kernels for 0%

profile of v1, /device:TPU:4, one launch (start us, length us, event | category | flops | bytes accessed | tf_op | source)
XLA Modules:
  0.0 717.8 jit_solution(9066870788544439)
XLA Ops:
  7.3 38.2 %all-gather.11.cloned.1.call-done = bf16[4,256,720]{1,2,0:T(8,128)(2,1)} async-done(((bf16[1,256,720]{1,2,0:T(8,128)(2,1)}), bf16[4,256,720]{1,2,0:T(8,128)(2,1)}) %all-gather.11.cloned.1.call-update) | async-done | bytes 1474576 | tf_op jit(solution)/shard_map/all_gather | solution.py:49
  45.5 3.5 convolution_bitcast_fusion
  49.1 25.1 %all-reduce.1 = bf16[256,720]{0,1:T(8,128)(2,1)} all-reduce(f32[256,720]{0,1:T(8,128)} %convolution_bitcast_fusion), channel_id=1, replica_groups=mesh['segment'=4,'ctx'=32,'head'=4] {'head'}, use_global_device_ids=true, to_apply=%region_1.0 | all-reduce | flops 184320 | bytes 1105920 | tf_op jit(solution)/shard_map/psum | solution.py:54
  78.9 14.9 %all-to-all-start = ((bf16[32,180,64]{1,2,0:T(8,128)(2,1)}), bf16[32,180,64]{1,2,0:T(8,128)(2,1)}, u32[]{:S(2)}, u32[]{:S(2)}) async-start(bf16[32,180,64]{1,2,0:T(8,128)(2,1)} %stack.2), calls=%async_computation | async-start | bytes 2097152 | tf_op jit(solution)/shard_map/all_to_all | solution.py:69
  94.4 115.0 %all-gather.3 = bf16[32,180,64]{1,2,0:T(8,128)(2,1)S(1)} all-gather(bf16[1,180,64]{1,2,0:T(8,128)(2,1)S(1)} %bitcast.58), channel_id=1, replica_groups=mesh['segment'=4,'ctx'=32,'head'=4] {'ctx'}, dimensions={0}, use_global_device_ids=true | all-gather | bytes 760320 | tf_op jit(solution)/shard_map/all_gather | solution.py:71
  211.0 3.1 reshape.162
  214.2 3.4 reshape.163
  217.6 2.2 multiply_reduce_fusion
  219.8 32.1 %multiply_reduce_fusion.1 = (f32[256]{0:T(256)S(1)}, f32[256,2880]{0,1:T(8,128)}) fusion(bf16[1,256,2880]{1,0,2:T(2,128)(2,1)} %all-gather.17.cloned.1.call-done), kind=kLoop, calls=%fused_computation.39 | loop fusion | flops 2211584 | bytes 4424704 | tf_op jit(solution)/shard_map/reduce_sum | solution.py:12
  253.3 4.0 reshape.151
  257.4 3.8 copy.26
  261.2 4.1 reshape.150
  270.2 2.8 copy.28
  273.0 3.2 reshape.148
  276.1 3.3 convolution_convert_fusion.2
  279.6 65.8 %all-gather.21.cloned.1.call-done = bf16[32,180,128]{2,1,0:T(8,128)(2,1)} async-done(((bf16[1,180,128]{2,1,0:T(8,128)(2,1)}), bf16[32,180,128]{2,1,0:T(8,128)(2,1)}) %all-gather.21.cloned.1.call-update) | async-done | bytes 1474576 | tf_op jit(solution)/shard_map/all_gather | solution.py:67
  345.4 3.3 reshape.160
  348.7 3.0 convolution_convert_fusion
  351.7 126.5 %all-gather.15.cloned.1.call-done = bf16[8192,64]{0,1:T(8,128)(2,1)} async-done(((bf16[256,64]{0,1:T(8,128)(2,1)}), bf16[8192,64]{0,1:T(8,128)(2,1)}) %all-gather.15.cloned.1.call-update) | async-done | bytes 1048592 | tf_op jit(solution)/shard_map/all_gather | solution.py:89
  478.3 132.5 %all-gather.13.cloned.1.call-done = bf16[8192,64]{0,1:T(8,128)(2,1)} async-done(((bf16[256,64]{0,1:T(8,128)(2,1)}), bf16[8192,64]{0,1:T(8,128)(2,1)}) %all-gather.13.cloned.1.call-update) | async-done | bytes 1048592 | tf_op jit(solution)/shard_map/all_gather | solution.py:88
  611.5 97.8 %while.20 = (s32[]{:T(128)}, f32[256,2]{0,1:T(2,128)S(1)}, f32[256,2]{0,1:T(2,128)S(1)}, f32[256,128]{0,1:T(8,128)}, s32[64]{0:T(128)S(1)}, /*index=5*/s32[256]{...) while((s32[]{:T(128)}, f32[256,2]{0,1:T(2,128)S(1)}, ...), condition=%wide.region_8.9_spmd.clone, body=%wide.region_4.8_spmd.clone.sunk | while | flops 69780480 | bytes 4175302 | solution.py:102
  615.3 2.2 convolution_add_fusion.2
  621.5 2.2 convolution_add_fusion.2
  627.6 2.2 convolution_add_fusion.2
  (207 shorter events, 107.3 us)
Async XLA Ops:
  6.5 39.0 %copy-start = (bf16[3,720,720]{2,1,0:T(8,128)(2,1)S(1)}, bf16[3,720,720]{2,1,0:T(8,128)(2,1)}, u32[]{:S(2)}) copy-start(bf16[3,720,720]{2,1,0:T(8,128)(2,1)} %param.9) | copy-start | bytes 9331204
  6.5 39.0 %all-gather.11.cloned.1.call-start = ((), (), s32[]{:S(2)}) async-start(), calls=%async_computation.1 | async-start | bytes 1843200 | tf_op jit(solution)/shard_map/all_gather | solution.py:49
  7.3 206.9 %all-gather.19.cloned.1.call-start = ((), (), s32[]{:S(2)}) async-start(), calls=%async_computation.5 | async-start | bytes 1601536 | tf_op jit(solution)/shard_map/all_gather | solution.py:59
  7.3 70.4 %copy-start.5 = (bf16[180,64]{0,1:T(8,128)(2,1)S(1)}, bf16[180,64]{0,1:T(8,128)(2,1)}, u32[]{:S(2)}) copy-start(bf16[180,64]{0,1:T(8,128)(2,1)} %param.11) | copy-start | bytes 69124
  49.1 45.3 %copy-start.6 = (bf16[180,64]{0,1:T(8,128)(2,1)S(1)}, bf16[180,64]{0,1:T(8,128)(2,1)}, u32[]{:S(2)}) copy-start(bf16[180,64]{0,1:T(8,128)(2,1)} %param.12) | copy-start | bytes 69124
  75.8 144.0 %all-gather.17.cloned.1.call-start = ((), (), s32[]{:S(2)}) async-start(), calls=%async_computation.4 | async-start | bytes 3133440 | tf_op jit(solution)/shard_map/all_gather | solution.py:60
  78.9 191.3 %all-to-all-start = ((bf16[32,180,64]{1,2,0:T(8,128)(2,1)}), bf16[32,180,64]{1,2,0:T(8,128)(2,1)}, u32[]{:S(2)}, u32[]{:S(2)}) async-start(bf16[32,180,64]{1,2,0:T(8,128)(2,1)} %stack.2), calls=%async_computation | async-start | bytes 2097152 | tf_op jit(solution)/shard_map/all_to_all | solution.py:69
  93.8 251.6 %all-gather.21.cloned.1.call-start = ((), (), s32[]{:S(2)}) async-start(), calls=%async_computation.6 | async-start | bytes 1554432 | tf_op jit(solution)/shard_map/all_gather | solution.py:67
  94.4 383.9 %all-gather.15.cloned.1.call-start = ((), (), s32[]{:S(2)}) async-start(), calls=%async_computation.3 | async-start | bytes 1081344 | tf_op jit(solution)/shard_map/all_gather | solution.py:89
  219.8 32.1 %copy-start.1 = (f32[2880,256]{1,0:T(8,128)S(1)}, f32[2880,256]{1,0:T(8,128)}, u32[]{:S(2)}) copy-start(f32[2880,256]{1,0:T(8,128)} %reshape.163) | copy-start | bytes 8847364
  265.3 3.4 copy-start.2
  265.3 3.4 copy-start.4
  267.5 1.1 copy-start.3
  269.9 340.9 %all-gather.13.cloned.1.call-start = ((), (), s32[]{:S(2)}) async-start(), calls=%async_computation.2 | async-start | bytes 1081344 | tf_op jit(solution)/shard_map/all_gather | solution.py:88
  276.1 3.4 copy-start.7
Sparse Core Ops, SparseCore 0:
  9.5 36.0 all-gather.10
  75.9 55.6 all-gather.18
  133.7 58.7 all-gather.16
  195.5 149.8 all-gather.20
  348.2 130.0 all-gather.14
  481.0 129.7 all-gather.12
